TPU v7x, 256 devices: a whole 4x4x8 slice. The times are simulated.
256 devices in a mesh: row: 32 (over z, x), col: 8 (over y, core).
Axes of the slice: x: 4, y: 4, z: 8, core: 2. Of those that a mesh axis runs over, the one named last changes fastest.
Arguments:
- image: bfloat16 [512, 1024, 256], P('row', 'col'), may hold values from -6 to 6
- kernel_one: bfloat16 [3, 3, 256, 256], replicated, may hold values from -0.125 to 0.125
- kernel_two: bfloat16 [3, 3, 256, 512], replicated, may hold values from -0.125 to 0.125
- cotangent: bfloat16 [256, 512, 512], P('row', 'col'), may hold values from -6 to 6
Outputs:
- image_grad: bfloat16 [512, 1024, 256], P('row', 'col')
- update_one: bfloat16 [3, 3, 256, 256], replicated
- update_two: bfloat16 [3, 3, 256, 512], replicated
All inputs are finite; a program needn't handle non-finite values.
Results may differ from a plain program's by a relative error of at most 0.006.
Values may be sent and summed in bfloat16 or wider, within the bound.
A program may use at most 128 MiB of HBM per device.

v0:
```python
import jax
import jax.numpy as jnp
from jax import lax
from jax.sharding import PartitionSpec as P


def padded(shard, sides, width):
    for axis, dim in sides:
        size, length = (lax.axis_size(axis), shard.shape[dim])
        up = [(i, (i + 1) % size) for i in range(size - 1)]
        down = [(j, i) for i, j in up]
        last = lax.slice_in_dim(shard, length - width, length, axis=dim)
        initial = lax.slice_in_dim(shard, 0, width, axis=dim)
        before = lax.ppermute(last, axis, up)
        after = lax.ppermute(initial, axis, down)
        shard = jnp.concatenate([before, shard, after], axis=dim)
    return shard


def passed_along(shard, axis, by):
    size = lax.axis_size(axis)
    pairs = [(i, i + by) for i in range(size) if 0 <= i + by < size]
    return lax.ppermute(shard, axis, pairs)


def conv_local(source, kernel, padding, dilation, layout):
    result = lax.conv_general_dilated(
        source[None],
        kernel,
        (1, 1),
        padding,
        lhs_dilation=dilation,
        dimension_numbers=("NHWC", layout, "NHWC"),
        preferred_element_type=jnp.float32,
    )
    return result[0]


def on_device(image, kernel_one, kernel_two, cotangent):
    rows_here = image.shape[0]
    cols_here = image.shape[1]
    image_pad = padded(image, (("row", 0), ("col", 1)), 1)
    pre_act = conv_local(image_pad, kernel_one, "VALID", (1, 1), "HWIO")
    activ = jax.nn.silu(pre_act).astype(jnp.bfloat16)
    left_edge = passed_along(activ[:, -1:], "col", 1)
    act_cols = jnp.concatenate([left_edge, activ], 1)
    top_edge = passed_along(act_cols[-1:], "row", 1)
    act_pad = jnp.concatenate([top_edge, act_cols], 0)
    rows_two = []
    for row_off in range(3):
        cols_two = []
        for col_off in range(3):
            patch = act_pad[
                row_off : row_off + rows_here - 1 : 2, col_off : col_off + cols_here - 1 : 2
            ]
            cols_two.append(
                jnp.einsum("ijc,ije->ce", patch, cotangent, preferred_element_type=jnp.float32)
            )
        rows_two.append(jnp.stack(cols_two))
    grad_two = jnp.stack(rows_two)
    flipped_two = kernel_two[::-1, ::-1]
    act_full = conv_local(cotangent, flipped_two, ((2, 2), (2, 2)), (2, 2), "HWOI")
    from_right = passed_along(act_full[:, :1], "col", -1)
    act_trim = act_full[:, 1:]
    act_trim = jnp.concatenate([act_trim[:, :-1], act_trim[:, -1:] + from_right], 1)
    from_below = passed_along(act_trim[:1].astype(jnp.bfloat16), "row", -1).astype(jnp.float32)
    act_grad = act_trim[1:]
    act_grad = jnp.concatenate([act_grad[:-1], act_grad[-1:] + from_below], 0)
    sig = jax.nn.sigmoid(pre_act)
    pre_grad = (act_grad * sig * (1.0 + pre_act * (1.0 - sig))).astype(jnp.bfloat16)
    rows_one = []
    for row_off in range(3):
        cols_one = []
        for col_off in range(3):
            patch = image_pad[row_off : row_off + rows_here, col_off : col_off + cols_here]
            cols_one.append(
                jnp.einsum("ijc,ijd->cd", patch, pre_grad, preferred_element_type=jnp.float32)
            )
        rows_one.append(jnp.stack(cols_one))
    grad_one = jnp.stack(rows_one)
    grad_pad = padded(pre_grad, (("row", 0), ("col", 1)), 1)
    image_grad = conv_local(grad_pad, kernel_one[::-1, ::-1], "VALID", (1, 1), "HWOI").astype(
        jnp.bfloat16
    )
    flat_one = grad_one.reshape(-1)
    flat_two = grad_two.reshape(-1)
    total_one, total_two = lax.psum((flat_one, flat_two), ("row", "col"))
    update_one = (total_one * lax.rsqrt(jnp.mean(total_one * total_one) + 1e-06)).astype(
        jnp.bfloat16
    )
    update_two = (total_two * lax.rsqrt(jnp.mean(total_two * total_two) + 1e-06)).astype(
        jnp.bfloat16
    )
    return (image_grad, update_one.reshape(kernel_one.shape), update_two.reshape(kernel_two.shape))


def solution(mesh):
    placed = (P("row", "col", None), P(), P(), P("row", "col", None))
    return jax.shard_map(
        on_device,
        mesh=mesh,
        in_specs=placed,
        out_specs=(P("row", "col", None), P(), P()),
        check_vma=False,
    )
```

profile of v0, /device:TPU:2, one launch (start us, length us, event | category | flops | bytes accessed | tf_op | source)
XLA Modules:
  0.0 440.2 jit_solution(7343728317577428346)
XLA Ops:
  7.2 1.5 copy.73
  9.0 1.7 convolution_select_fusion
  10.7 2.6 copy.37
  13.3 4.1 reshape.29
  17.4 1.9 slice_bitcast_fusion
  19.4 1.4 copy-done.4
  20.8 1.3 collective-permute-start
  22.8 3.4 collective-permute-start.2
  26.2 2.4 collective-permute-start.3
  28.6 1.9 slice.155
  31.5 1.5 fusion.4
  33.2 1.9 fusion.54
  35.0 1.8 copy.41
  36.8 2.5 collective-permute-start.4
  39.3 1.8 copy.42
  41.1 1.3 collective-permute-start.5
  43.1 1.9 collective-permute-start.1
  45.0 1.5 copy.43
  46.5 1.5 copy.44
  47.9 4.4 maximum_bitcast_fusion
  52.3 3.9 copy.64
  56.2 2.5 pad.2.clone
  58.6 3.2 reshape.32
  61.9 1.9 copy.47
  63.8 3.0 convolution_select_fusion.1
  66.9 3.6 maximum_maximum_fusion
  71.4 1.5 copy-done.5
  72.9 1.8 multiply_convert_fusion.2
  74.7 2.7 slice.143
  77.4 2.7 slice.142
  80.1 2.7 slice.146
  82.8 2.7 slice.145
  85.5 1.8 convolution_bitcast_fusion.15
  91.0 4.4 %collective-permute-start.10 = (bf16[16,1,256]{2,1,0:T(2,128)(2,1)S(1)}, bf16[16,1,256]{2,1,0:T(2,128)(2,1)S(1)}, u32[]{:S(2)}, u32[]{:S(2)}) collective-permute-start(bf16[16,1,256]{2,1,0:T(2,128)(2,1)S(1)} %slice.178), channel_id=1, source_target_pairs={{0,1},{1,2},{2,3},{3,4},{4,5},{5,6},{6,7},{8,9},{9,10},{10,11},{11... | collective-permute-start | bytes 24584 | tf_op jit(solution)/shard_map/ppermute | solution.py:23
  95.5 1.1 convolution_bitcast_fusion.3
  96.6 1.1 convolution_bitcast_fusion.4
  101.3 2.6 copy.65
  104.3 2.7 slice.141
  107.5 3.8 collective-permute-start.11
  111.3 2.3 convolution_bitcast_fusion.5
  113.9 1.3 maximum_bitcast_fusion.3
  115.7 2.7 slice.140
  118.4 2.7 slice.139
  121.5 1.5 convolution_bitcast_fusion.6
  123.1 1.4 convolution_bitcast_fusion.7
  124.5 1.4 convolution_bitcast_fusion.8
  127.9 3.4 copy.66
  131.3 4.7 %collective-permute-start.6 = (bf16[1,128,256]{2,1,0:T(8,128)(2,1)S(1)}, bf16[1,128,256]{2,1,0:T(8,128)(2,1)S(1)}, u32[]{:S(2)}, u32[]{:S(2)}) collective-permute-start(bf16[1,128,256]{2,1,0:T(8,128)(2,1)S(1)} %get-tuple-element.19), channel_id=1, source_target_pairs={{0,8},{8,16},{16,24},{24,32},{32,40},{40,48},{48,56},{56,64},{64,7... | collective-permute-start | bytes 196616 | tf_op jit(solution)/shard_map/ppermute | solution.py:14
  135.9 1.9 collective-permute-start.7
  138.0 5.9 %collective-permute-done.7 = bf16[1,128,256]{2,1,0:T(8,128)(2,1)S(1)} collective-permute-done((bf16[1,128,256]{2,1,0:T(8,128)(2,1)S(1)}, bf16[1,128,256]{2,1,0:T(8,128)(2,1)S(1)}, u32[]{:S(2)}, u32[]{:S(2)}) %collective-permute-start.7) | collective-permute-done | bytes 65568 | tf_op jit(solution)/shard_map/ppermute | solution.py:15
  143.9 2.5 collective-permute-start.8
  146.4 1.6 collective-permute-start.9
  148.0 3.1 collective-permute-done.9
  151.9 1.2 pad.4
  153.1 2.3 reshape.39
  156.7 2.8 select_convert_fusion
  159.8 1.3 copy.59
  161.1 255.9 %all-reduce.3.cloned.1.call-done = (f32[589824]{0:T(1024)}, f32[1179648]{0:T(1024)}) async-done(((f32[589824]{0:T(1024)}, f32[1179648]{0:T(1024)}), (f32[589824]{0:T(1024)}, f32[1179648]{0:T(1024)})) %all-reduce.3.cloned.1.call-update) | async-done | bytes 7077904 | tf_op jit(solution)/shard_map/psum | solution.py:87
  417.1 3.6 multiply_reduce_fusion
  421.3 2.5 multiply_convert_fusion
  423.9 2.7 reshape.22
  426.6 2.9 multiply_reduce_fusion.1
  430.2 1.9 multiply_convert_fusion.1
  432.1 1.2 reshape.20
  (108 shorter events, 17.3 us)
Async XLA Ops:
  7.2 1.8 copy-start
  7.2 1.8 copy-start.27
  7.2 409.9 %all-reduce.3.cloned.1.call-start = ((), (), s32[]{:S(2)}) async-start(), calls=%async_computation | async-start | bytes 14155776 | tf_op jit(solution)/shard_map/psum | solution.py:87
  17.4 4.7 %copy-start.9 = (bf16[16,128,256]{2,1,0:T(8,128)(2,1)S(1)}, bf16[16,128,256]{2,1,0:T(8,128)(2,1)}, u32[]{:S(2)}) copy-start(bf16[16,128,256]{2,1,0:T(8,128)(2,1)} %param.4) | copy-start | bytes 3145732
  19.3 1.4 copy-start.4
  20.8 9.8 %collective-permute-start = (f32[17,1,256]{2,1,0:T(1,128)S(1)}, f32[17,1,256]{2,1,0:T(1,128)S(1)}, u32[]{:S(2)}, u32[]{:S(2)}) collective-permute-start(f32[17,1,256]{2,1,0:T(1,128)S(1)} %slice.157), channel_id=1, source_target_pairs={{1,0},{2,1},{3,2},{4,3},{5,4},{6,5},{7,6},{9,8},{10,9},{11,10},{12... | collective-permute-start | bytes 52232 | tf_op jit(solution)/shard_map/ppermute | solution.py:23
  22.8 10.2 %collective-permute-start.2 = (bf16[1,128,256]{1,2,0:T(8,128)(2,1)S(1)}, bf16[1,128,256]{1,2,0:T(8,128)(2,1)S(1)}, u32[]{:S(2)}, u32[]{:S(2)}) collective-permute-start(bf16[1,128,256]{1,2,0:T(8,128)(2,1)S(1)} %get-tuple-element.21), channel_id=1, source_target_pairs={{0,8},{8,16},{16,24},{24,32},{32,40},{40,48},{48,56},{56,64},{64,7... | collective-permute-start | bytes 196616 | tf_op jit(solution)/shard_map/ppermute | solution.py:14
  26.2 6.8 %collective-permute-start.3 = (bf16[1,128,256]{1,2,0:T(8,128)(2,1)S(1)}, bf16[1,128,256]{1,2,0:T(8,128)(2,1)S(1)}, u32[]{:S(2)}, u32[]{:S(2)}) collective-permute-start(bf16[1,128,256]{1,2,0:T(8,128)(2,1)S(1)} %get-tuple-element.22), channel_id=1, source_target_pairs={{8,0},{16,8},{24,16},{32,24},{40,32},{48,40},{56,48},{64,56},{72,6... | collective-permute-start | bytes 196616 | tf_op jit(solution)/shard_map/ppermute | solution.py:15
  36.8 8.1 %collective-permute-start.4 = (bf16[18,1,256]{2,0,1:T(8,128)(2,1)S(1)}, bf16[18,1,256]{2,0,1:T(8,128)(2,1)S(1)}, u32[]{:S(2)}, u32[]{:S(2)}) collective-permute-start(bf16[18,1,256]{2,0,1:T(8,128)(2,1)S(1)} %copy.41), channel_id=1, source_target_pairs={{0,1},{1,2},{2,3},{3,4},{4,5},{5,6},{6,7},{8,9},{9,10},{10,11},{11... | collective-permute-start | bytes 27656 | tf_op jit(solution)/shard_map/ppermute | solution.py:14
  41.1 5.4 %collective-permute-start.5 = (bf16[18,1,256]{2,0,1:T(8,128)(2,1)S(1)}, bf16[18,1,256]{2,0,1:T(8,128)(2,1)S(1)}, u32[]{:S(2)}, u32[]{:S(2)}) collective-permute-start(bf16[18,1,256]{2,0,1:T(8,128)(2,1)S(1)} %copy.42), channel_id=1, source_target_pairs={{1,0},{2,1},{3,2},{4,3},{5,4},{6,5},{7,6},{9,8},{10,9},{11,10},{12... | collective-permute-start | bytes 27656 | tf_op jit(solution)/shard_map/ppermute | solution.py:15
  43.1 28.3 %collective-permute-start.1 = (bf16[1,128,256]{2,1,0:T(8,128)(2,1)}, bf16[1,128,256]{2,1,0:T(8,128)(2,1)S(1)}, u32[]{:S(2)}, u32[]{:S(2)}) collective-permute-start(bf16[1,128,256]{2,1,0:T(8,128)(2,1)} %fusion.41), channel_id=1, source_target_pairs={{8,0},{16,8},{24,16},{32,24},{40,32},{48,40},{56,48},{64,56},{72,6... | collective-permute-start | bytes 196616 | tf_op jit(solution)/shard_map/ppermute | solution.py:23
  61.9 1.9 copy-start.24
  61.9 1.9 copy-start.26
  63.8 3.0 copy-start.2
  63.8 3.0 copy-start.3
  71.3 1.5 copy-start.5
  85.5 2.0 copy-start.8
  85.5 2.7 copy-start.7
  88.2 1.2 copy-start.10
  90.0 5.5 %copy-start.14 = (bf16[8,64,512]{2,1,0:T(8,128)(2,1)S(1)}, bf16[8,64,512]{2,1,0:T(8,128)(2,1)}, u32[]{:S(2)}) copy-start(bf16[8,64,512]{2,1,0:T(8,128)(2,1)} %param.7) | copy-start | bytes 1572868
  90.0 5.5 %copy-start.21 = (bf16[8,64,256]{2,1,0:T(8,128)(2,1)S(1)}, bf16[8,64,256]{2,1,0:T(8,128)(2,1)}, u32[]{:S(2)}) copy-start(bf16[8,64,256]{2,1,0:T(8,128)(2,1)} %slice.143) | copy-start | bytes 786436
  90.4 6.2 %copy-start.20 = (bf16[8,64,256]{2,1,0:T(8,128)(2,1)S(1)}, bf16[8,64,256]{2,1,0:T(8,128)(2,1)}, u32[]{:S(2)}) copy-start(bf16[8,64,256]{2,1,0:T(8,128)(2,1)} %slice.142) | copy-start | bytes 786436
  91.0 6.8 %copy-start.19 = (bf16[8,64,256]{2,1,0:T(8,128)(2,1)S(1)}, bf16[8,64,256]{2,1,0:T(8,128)(2,1)}, u32[]{:S(2)}) copy-start(bf16[8,64,256]{2,1,0:T(8,128)(2,1)} %slice.146) | copy-start | bytes 786436
  91.0 7.9 %copy-start.18 = (bf16[8,64,256]{2,1,0:T(8,128)(2,1)S(1)}, bf16[8,64,256]{2,1,0:T(8,128)(2,1)}, u32[]{:S(2)}) copy-start(bf16[8,64,256]{2,1,0:T(8,128)(2,1)} %slice.145) | copy-start | bytes 786436
  91.0 12.9 %collective-permute-start.10 = (bf16[16,1,256]{2,1,0:T(2,128)(2,1)S(1)}, bf16[16,1,256]{2,1,0:T(2,128)(2,1)S(1)}, u32[]{:S(2)}, u32[]{:S(2)}) collective-permute-start(bf16[16,1,256]{2,1,0:T(2,128)(2,1)S(1)} %slice.178), channel_id=1, source_target_pairs={{0,1},{1,2},{2,3},{3,4},{4,5},{5,6},{6,7},{8,9},{9,10},{10,11},{11... | collective-permute-start | bytes 24584 | tf_op jit(solution)/shard_map/ppermute | solution.py:23
  103.9 9.7 %copy-start.22 = (bf16[16,1,256]{2,1,0:T(2,128)(2,1)}, bf16[16,1,256]{2,1,0:T(2,128)(2,1)S(1)}, u32[]{:S(2)}) copy-start(bf16[16,1,256]{2,1,0:T(2,128)(2,1)S(1)} %collective-permute-done.10) | copy-start | bytes 24580
  107.5 6.1 %copy-start.15 = (bf16[8,64,512]{2,1,0:T(8,128)(2,1)S(1)}, bf16[8,64,512]{2,1,0:T(8,128)(2,1)}, u32[]{:S(2)}) copy-start(bf16[8,64,512]{2,1,0:T(8,128)(2,1)} %param.7) | copy-start | bytes 1572868
  107.5 6.4 %copy-start.16 = (f32[1,256,512]{2,1,0:T(8,128)S(1)}, f32[1,256,512]{2,1,0:T(8,128)}, u32[]{:S(2)}) copy-start(f32[1,256,512]{2,1,0:T(8,128)} %convolution_bitcast_fusion) | copy-start | bytes 1572868
  107.5 6.4 %copy-start.17 = (f32[1,256,512]{2,1,0:T(8,128)S(1)}, f32[1,256,512]{2,1,0:T(8,128)}, u32[]{:S(2)}) copy-start(f32[1,256,512]{2,1,0:T(8,128)} %convolution_bitcast_fusion.1) | copy-start | bytes 1572868
  107.5 7.7 %collective-permute-start.11 = (bf16[1,129,256]{2,1,0:T(8,128)(2,1)S(1)}, bf16[1,129,256]{2,1,0:T(8,128)(2,1)S(1)}, u32[]{:S(2)}, u32[]{:S(2)}) collective-permute-start(bf16[1,129,256]{2,1,0:T(8,128)(2,1)S(1)} %fusion.42), channel_id=1, source_target_pairs={{0,8},{8,16},{16,24},{24,32},{32,40},{40,48},{48,56},{56,64},{64,7... | collective-permute-start | bytes 198152 | tf_op jit(solution)/shard_map/ppermute | solution.py:23
  113.9 1.3 copy-start.23
  121.5 4.4 copy-start.11
  121.5 4.4 copy-start.12
  121.5 4.4 copy-start.13
  125.9 1.4 copy-start.6
  131.3 6.7 %collective-permute-start.6 = (bf16[1,128,256]{2,1,0:T(8,128)(2,1)S(1)}, bf16[1,128,256]{2,1,0:T(8,128)(2,1)S(1)}, u32[]{:S(2)}, u32[]{:S(2)}) collective-permute-start(bf16[1,128,256]{2,1,0:T(8,128)(2,1)S(1)} %get-tuple-element.19), channel_id=1, source_target_pairs={{0,8},{8,16},{16,24},{24,32},{32,40},{40,48},{48,56},{56,64},{64,7... | collective-permute-start | bytes 196616 | tf_op jit(solution)/shard_map/ppermute | solution.py:14
  135.9 8.0 %collective-permute-start.7 = (bf16[1,128,256]{2,1,0:T(8,128)(2,1)S(1)}, bf16[1,128,256]{2,1,0:T(8,128)(2,1)S(1)}, u32[]{:S(2)}, u32[]{:S(2)}) collective-permute-start(bf16[1,128,256]{2,1,0:T(8,128)(2,1)S(1)} %get-tuple-element.20), channel_id=1, source_target_pairs={{8,0},{16,8},{24,16},{32,24},{40,32},{48,40},{56,48},{64,56},{72,6... | collective-permute-start | bytes 196616 | tf_op jit(solution)/shard_map/ppermute | solution.py:15
  143.9 4.1 collective-permute-start.8
  146.4 4.7 %collective-permute-start.9 = (bf16[18,1,256]{2,1,0:T(2,128)(2,1)S(1)}, bf16[18,1,256]{2,1,0:T(2,128)(2,1)S(1)}, u32[]{:S(2)}, u32[]{:S(2)}) collective-permute-start(bf16[18,1,256]{2,1,0:T(2,128)(2,1)S(1)} %get-tuple-element.16), channel_id=1, source_target_pairs={{1,0},{2,1},{3,2},{4,3},{5,4},{6,5},{7,6},{9,8},{10,9},{11,10},{12... | collective-permute-start | bytes 27656 | tf_op jit(solution)/shard_map/ppermute | solution.py:15
  155.4 1.3 copy-start.25
  430.1 3.2 copy-start.1
Sparse Core Ops, SparseCore 0:
  131.4 285.6 all-reduce.2
where the time goes:
time: 441 us; the launch traced here: 440 us
  waiting for transfers between devices  265 us (60%)
  local copies, waits for them, and re-layouts  74.5 us (17%)
  starting transfers between devices  31.7 us (7%)
  other arithmetic  28 us (6%)
  matrix products  24.6 us (6%)
  between operations  16.2 us (4%)
    psum x1, waiting for transfers between devices, on_device(): total_one, total_two = lax.psum((flat_one, flat_two), ('row', 'col'))  256 us
    slice x9, local copies, waits for them, and re-layouts, on_device(): act_pad[row_off:row_off + rows_here - 1:2, col_off:col_off + cols_here -...  19.8 us
    unnamed x62, local copies, waits for them, and re-layouts  18.9 us
    conv_general_dilated x12, local copies, waits for them, and re-layouts, conv_local(): lax.conv_general_dilated(source[None], kernel, (1, 1), padding, lhs_dilat...  15.6 us
    ppermute x4, starting transfers between devices, padded(): before = lax.ppermute(last, axis, up)  13 us
    dot_general x9, matrix products, on_device(): jnp.einsum('ijc,ije->ce', patch, cotangent, preferred_element_type=jnp.fl...  11.4 us
    ppermute x4, starting transfers between devices, passed_along(): return lax.ppermute(shard, axis, pairs)  11.4 us
    ppermute x4, waiting for transfers between devices, padded(): after = lax.ppermute(initial, axis, down)  9.07 us
  transfers between devices with their start and end apart: 13, of which 4 were waited for; matrix products, arithmetic and copies ran while one was open for 12% of the time, Pallas kernels for 0%

commit v1 on v0

--- a/solution.py
+++ b/solution.py
@@ -2,6 +2,11 @@
 import jax.numpy as jnp
 from jax import lax
 from jax.sharding import PartitionSpec as P
+
+
+def axis_by_axis(value, first, second):
+    inner = lax.psum(value, first)
+    return lax.psum(inner, second)
 
 
 def padded(shard, sides, width):
@@ -84,7 +89,7 @@
     )
     flat_one = grad_one.reshape(-1)
     flat_two = grad_two.reshape(-1)
-    total_one, total_two = lax.psum((flat_one, flat_two), ("row", "col"))
+    total_one, total_two = axis_by_axis((flat_one, flat_two), "col", "row")
     update_one = (total_one * lax.rsqrt(jnp.mean(total_one * total_one) + 1e-06)).astype(
         jnp.bfloat16
     )

time: 441 us -> 461 us (1.045)
  waiting for transfers between devices: 265 us -> 286 us
    psum x1 -> x2, waiting for transfers between devices: 256 us -> 281 us  [the longest x1 174 us: axis_by_axis(): return lax.psum(inner, second)]
  transfers between devices with their start and end apart: 13 -> 14, of which waited for: 4 -> 5; matrix products, arithmetic and copies ran while one was open for 12% -> 12% of each run, Pallas kernels for 0% -> 0%
where the time goes in v1:
time: 461 us; the launch traced here: 459 us
  waiting for transfers between devices  286 us (62%)
  local copies, waits for them, and re-layouts  74.5 us (16%)
  starting transfers between devices  29.8 us (6%)
  other arithmetic  28.1 us (6%)
  matrix products  24.6 us (5%)
  between operations  16.2 us (4%)
    psum x1, waiting for transfers between devices, axis_by_axis(): return lax.psum(inner, second)  174 us
    psum x1, waiting for transfers between devices, axis_by_axis(): inner = lax.psum(value, first)  107 us
    slice x9, local copies, waits for them, and re-layouts, on_device(): act_pad[row_off:row_off + rows_here - 1:2, col_off:col_off + cols_here -...  19.8 us
    unnamed x62, local copies, waits for them, and re-layouts  19 us
    conv_general_dilated x12, local copies, waits for them, and re-layouts, conv_local(): lax.conv_general_dilated(source[None], kernel, (1, 1), padding, lhs_dilat...  15.6 us
    dot_general x9, matrix products, on_device(): jnp.einsum('ijc,ije->ce', patch, cotangent, preferred_element_type=jnp.fl...  11.4 us
    ppermute x4, starting transfers between devices, passed_along(): return lax.ppermute(shard, axis, pairs)  11.4 us
    ppermute x4, starting transfers between devices, padded(): before = lax.ppermute(last, axis, up)  10.5 us
  transfers between devices with their start and end apart: 14, of which 5 were waited for; matrix products, arithmetic and copies ran while one was open for 12% of the time, Pallas kernels for 0%

profile of v1, /device:TPU:2, one launch (start us, length us, event | category | flops | bytes accessed | tf_op | source)
XLA Modules:
  0.0 459.2 jit_solution(3829064986734693746)
XLA Ops:
  7.2 1.5 copy.73
  9.0 1.7 convolution_select_fusion
  10.7 2.6 copy.37
  13.3 4.1 reshape.29
  17.4 1.9 slice_bitcast_fusion
  19.4 1.4 copy-done.4
  20.8 1.3 collective-permute-start
  22.8 3.4 collective-permute-start.2
  26.2 2.4 collective-permute-start.3
  28.6 1.9 slice.155
  31.5 1.5 fusion.4
  33.2 1.9 fusion.54
  35.1 1.8 copy.41
  36.9 2.5 collective-permute-start.4
  39.3 1.8 copy.42
  41.1 1.3 collective-permute-start.5
  43.1 1.9 collective-permute-start.1
  45.0 1.5 copy.43
  46.5 1.5 copy.44
  48.0 4.4 maximum_bitcast_fusion
  52.3 3.9 copy.64
  56.2 2.4 pad.2.clone
  58.6 3.2 reshape.32
  61.9 1.9 copy.47
  63.9 3.0 convolution_select_fusion.1
  66.9 3.6 maximum_maximum_fusion
  71.5 1.5 copy-done.5
  73.0 1.8 multiply_convert_fusion.2
  74.8 2.7 slice.143
  77.5 2.7 slice.142
  80.1 2.7 slice.146
  82.9 2.7 slice.145
  85.6 1.8 convolution_bitcast_fusion.15
  91.1 4.4 collective-permute-start.10
  96.7 1.1 convolution_bitcast_fusion.4
  101.3 2.6 copy.65
  104.4 2.7 slice.141
  107.6 3.8 collective-permute-start.11
  111.4 2.3 convolution_bitcast_fusion.5
  114.0 1.3 maximum_bitcast_fusion.3
  115.7 2.7 slice.140
  118.5 2.7 slice.139
  121.6 1.5 convolution_bitcast_fusion.6
  123.2 1.4 convolution_bitcast_fusion.7
  124.6 1.4 convolution_bitcast_fusion.8
  127.9 3.4 copy.66
  131.4 106.7 %all-reduce.7.cloned.1.call-done = (f32[589824]{0:T(1024)}, f32[1179648]{0:T(1024)}) async-done(((f32[589824]{0:T(1024)}, f32[1179648]{0:T(1024)}), (f32[589824]{0:T(1024)}, f32[1179648]{0:T(1024)})) %all-reduce.7.cloned.1.call-update) | async-done | bytes 7077904 | tf_op jit(solution)/shard_map/psum | solution.py:8
  238.1 3.4 collective-permute-start.6
  241.5 2.5 collective-permute-start.7
  244.3 3.4 collective-permute-done.7
  247.7 1.3 collective-permute-start.8
  249.0 1.6 collective-permute-start.9
  250.5 1.7 collective-permute-done.9
  253.0 1.1 pad.4
  254.1 2.3 reshape.39
  257.7 2.8 select_convert_fusion
  260.8 1.3 copy.59
  262.1 174.0 %all-reduce.5.cloned.1.call-done = (f32[589824]{0:T(1024)}, f32[1179648]{0:T(1024)}) async-done(((f32[589824]{0:T(1024)}, f32[1179648]{0:T(1024)}), (f32[589824]{0:T(1024)}, f32[1179648]{0:T(1024)})) %all-reduce.5.cloned.1.call-update) | async-done | bytes 7077904 | tf_op jit(solution)/shard_map/psum | solution.py:9
  436.1 3.6 multiply_reduce_fusion
  440.4 2.5 multiply_convert_fusion
  442.9 2.7 reshape.22
  445.6 2.9 multiply_reduce_fusion.1
  449.2 1.9 multiply_convert_fusion.1
  451.1 1.2 reshape.20
  (111 shorter events, 18.6 us)
Async XLA Ops:
  7.2 1.8 copy-start
  7.2 1.8 copy-start.27
  7.2 230.9 %all-reduce.7.cloned.1.call-start = ((), (), s32[]{:S(2)}) async-start(), calls=%async_computation.1 | async-start | bytes 14155776 | tf_op jit(solution)/shard_map/psum | solution.py:8
  17.4 4.6 %copy-start.9 = (bf16[16,128,256]{2,1,0:T(8,128)(2,1)S(1)}, bf16[16,128,256]{2,1,0:T(8,128)(2,1)}, u32[]{:S(2)}) copy-start(bf16[16,128,256]{2,1,0:T(8,128)(2,1)} %param.4) | copy-start | bytes 3145732
  19.3 1.4 copy-start.4
  20.8 9.8 %collective-permute-start = (f32[17,1,256]{2,1,0:T(1,128)S(1)}, f32[17,1,256]{2,1,0:T(1,128)S(1)}, u32[]{:S(2)}, u32[]{:S(2)}) collective-permute-start(f32[17,1,256]{2,1,0:T(1,128)S(1)} %slice.157), channel_id=1, source_target_pairs={{1,0},{2,1},{3,2},{4,3},{5,4},{6,5},{7,6},{9,8},{10,9},{11,10},{12... | collective-permute-start | bytes 52232 | tf_op jit(solution)/shard_map/ppermute | solution.py:28
  22.8 10.2 %collective-permute-start.2 = (bf16[1,128,256]{1,2,0:T(8,128)(2,1)S(1)}, bf16[1,128,256]{1,2,0:T(8,128)(2,1)S(1)}, u32[]{:S(2)}, u32[]{:S(2)}) collective-permute-start(bf16[1,128,256]{1,2,0:T(8,128)(2,1)S(1)} %get-tuple-element.23), channel_id=1, source_target_pairs={{0,8},{8,16},{16,24},{24,32},{32,40},{40,48},{48,56},{56,64},{64,7... | collective-permute-start | bytes 196616 | tf_op jit(solution)/shard_map/ppermute | solution.py:19
  26.2 6.8 %collective-permute-start.3 = (bf16[1,128,256]{1,2,0:T(8,128)(2,1)S(1)}, bf16[1,128,256]{1,2,0:T(8,128)(2,1)S(1)}, u32[]{:S(2)}, u32[]{:S(2)}) collective-permute-start(bf16[1,128,256]{1,2,0:T(8,128)(2,1)S(1)} %get-tuple-element.24), channel_id=1, source_target_pairs={{8,0},{16,8},{24,16},{32,24},{40,32},{48,40},{56,48},{64,56},{72,6... | collective-permute-start | bytes 196616 | tf_op jit(solution)/shard_map/ppermute | solution.py:20
  36.9 8.1 %collective-permute-start.4 = (bf16[18,1,256]{2,0,1:T(8,128)(2,1)S(1)}, bf16[18,1,256]{2,0,1:T(8,128)(2,1)S(1)}, u32[]{:S(2)}, u32[]{:S(2)}) collective-permute-start(bf16[18,1,256]{2,0,1:T(8,128)(2,1)S(1)} %copy.41), channel_id=1, source_target_pairs={{0,1},{1,2},{2,3},{3,4},{4,5},{5,6},{6,7},{8,9},{9,10},{10,11},{11... | collective-permute-start | bytes 27656 | tf_op jit(solution)/shard_map/ppermute | solution.py:19
  41.1 5.4 %collective-permute-start.5 = (bf16[18,1,256]{2,0,1:T(8,128)(2,1)S(1)}, bf16[18,1,256]{2,0,1:T(8,128)(2,1)S(1)}, u32[]{:S(2)}, u32[]{:S(2)}) collective-permute-start(bf16[18,1,256]{2,0,1:T(8,128)(2,1)S(1)} %copy.42), channel_id=1, source_target_pairs={{1,0},{2,1},{3,2},{4,3},{5,4},{6,5},{7,6},{9,8},{10,9},{11,10},{12... | collective-permute-start | bytes 27656 | tf_op jit(solution)/shard_map/ppermute | solution.py:20
  43.1 28.4 %collective-permute-start.1 = (bf16[1,128,256]{2,1,0:T(8,128)(2,1)}, bf16[1,128,256]{2,1,0:T(8,128)(2,1)S(1)}, u32[]{:S(2)}, u32[]{:S(2)}) collective-permute-start(bf16[1,128,256]{2,1,0:T(8,128)(2,1)} %fusion.41), channel_id=1, source_target_pairs={{8,0},{16,8},{24,16},{32,24},{40,32},{48,40},{56,48},{64,56},{72,6... | collective-permute-start | bytes 196616 | tf_op jit(solution)/shard_map/ppermute | solution.py:28
  61.9 1.9 copy-start.24
  61.9 1.9 copy-start.26
  63.8 3.0 copy-start.2
  63.8 3.0 copy-start.3
  71.4 1.5 copy-start.5
  85.6 2.0 copy-start.8
  85.6 2.7 copy-start.7
  88.3 1.2 copy-start.10
  90.1 5.5 %copy-start.14 = (bf16[8,64,512]{2,1,0:T(8,128)(2,1)S(1)}, bf16[8,64,512]{2,1,0:T(8,128)(2,1)}, u32[]{:S(2)}) copy-start(bf16[8,64,512]{2,1,0:T(8,128)(2,1)} %param.7) | copy-start | bytes 1572868
  90.1 5.5 %copy-start.21 = (bf16[8,64,256]{2,1,0:T(8,128)(2,1)S(1)}, bf16[8,64,256]{2,1,0:T(8,128)(2,1)}, u32[]{:S(2)}) copy-start(bf16[8,64,256]{2,1,0:T(8,128)(2,1)} %slice.143) | copy-start | bytes 786436
  90.5 6.1 %copy-start.20 = (bf16[8,64,256]{2,1,0:T(8,128)(2,1)S(1)}, bf16[8,64,256]{2,1,0:T(8,128)(2,1)}, u32[]{:S(2)}) copy-start(bf16[8,64,256]{2,1,0:T(8,128)(2,1)} %slice.142) | copy-start | bytes 786436
  91.1 6.7 %copy-start.19 = (bf16[8,64,256]{2,1,0:T(8,128)(2,1)S(1)}, bf16[8,64,256]{2,1,0:T(8,128)(2,1)}, u32[]{:S(2)}) copy-start(bf16[8,64,256]{2,1,0:T(8,128)(2,1)} %slice.146) | copy-start | bytes 786436
  91.1 7.8 %copy-start.18 = (bf16[8,64,256]{2,1,0:T(8,128)(2,1)S(1)}, bf16[8,64,256]{2,1,0:T(8,128)(2,1)}, u32[]{:S(2)}) copy-start(bf16[8,64,256]{2,1,0:T(8,128)(2,1)} %slice.145) | copy-start | bytes 786436
  91.1 12.8 %collective-permute-start.10 = (bf16[16,1,256]{2,1,0:T(2,128)(2,1)S(1)}, bf16[16,1,256]{2,1,0:T(2,128)(2,1)S(1)}, u32[]{:S(2)}, u32[]{:S(2)}) collective-permute-start(bf16[16,1,256]{2,1,0:T(2,128)(2,1)S(1)} %slice.178), channel_id=1, source_target_pairs={{0,1},{1,2},{2,3},{3,4},{4,5},{5,6},{6,7},{8,9},{9,10},{10,11},{11... | collective-permute-start | bytes 24584 | tf_op jit(solution)/shard_map/ppermute | solution.py:28
  103.9 9.7 %copy-start.22 = (bf16[16,1,256]{2,1,0:T(2,128)(2,1)}, bf16[16,1,256]{2,1,0:T(2,128)(2,1)S(1)}, u32[]{:S(2)}) copy-start(bf16[16,1,256]{2,1,0:T(2,128)(2,1)S(1)} %collective-permute-done.10) | copy-start | bytes 24580
  107.5 6.1 %copy-start.15 = (bf16[8,64,512]{2,1,0:T(8,128)(2,1)S(1)}, bf16[8,64,512]{2,1,0:T(8,128)(2,1)}, u32[]{:S(2)}) copy-start(bf16[8,64,512]{2,1,0:T(8,128)(2,1)} %param.7) | copy-start | bytes 1572868
  107.5 6.4 %copy-start.16 = (f32[1,256,512]{2,1,0:T(8,128)S(1)}, f32[1,256,512]{2,1,0:T(8,128)}, u32[]{:S(2)}) copy-start(f32[1,256,512]{2,1,0:T(8,128)} %convolution_bitcast_fusion) | copy-start | bytes 1572868
  107.6 6.4 %copy-start.17 = (f32[1,256,512]{2,1,0:T(8,128)S(1)}, f32[1,256,512]{2,1,0:T(8,128)}, u32[]{:S(2)}) copy-start(f32[1,256,512]{2,1,0:T(8,128)} %convolution_bitcast_fusion.1) | copy-start | bytes 1572868
  107.6 7.7 %collective-permute-start.11 = (bf16[1,129,256]{2,1,0:T(8,128)(2,1)S(1)}, bf16[1,129,256]{2,1,0:T(8,128)(2,1)S(1)}, u32[]{:S(2)}, u32[]{:S(2)}) collective-permute-start(bf16[1,129,256]{2,1,0:T(8,128)(2,1)S(1)} %fusion.42), channel_id=1, source_target_pairs={{0,8},{8,16},{16,24},{24,32},{32,40},{40,48},{48,56},{56,64},{64,7... | collective-permute-start | bytes 198152 | tf_op jit(solution)/shard_map/ppermute | solution.py:28
  114.0 1.3 copy-start.23
  121.6 4.4 copy-start.11
  121.6 4.4 copy-start.12
  121.6 4.4 copy-start.13
  126.0 1.4 copy-start.6
  131.3 304.7 %all-reduce.5.cloned.1.call-start = ((), (), s32[]{:S(2)}) async-start(), calls=%async_computation | async-start | bytes 14155776 | tf_op jit(solution)/shard_map/psum | solution.py:9
  238.1 6.2 %collective-permute-start.6 = (bf16[1,128,256]{2,1,0:T(8,128)(2,1)S(1)}, bf16[1,128,256]{2,1,0:T(8,128)(2,1)S(1)}, u32[]{:S(2)}, u32[]{:S(2)}) collective-permute-start(bf16[1,128,256]{2,1,0:T(8,128)(2,1)S(1)} %get-tuple-element.21), channel_id=1, source_target_pairs={{0,8},{8,16},{16,24},{24,32},{32,40},{40,48},{48,56},{56,64},{64,7... | collective-permute-start | bytes 196616 | tf_op jit(solution)/shard_map/ppermute | solution.py:19
  241.5 6.2 %collective-permute-start.7 = (bf16[1,128,256]{2,1,0:T(8,128)(2,1)S(1)}, bf16[1,128,256]{2,1,0:T(8,128)(2,1)S(1)}, u32[]{:S(2)}, u32[]{:S(2)}) collective-permute-start(bf16[1,128,256]{2,1,0:T(8,128)(2,1)S(1)} %get-tuple-element.22), channel_id=1, source_target_pairs={{8,0},{16,8},{24,16},{32,24},{40,32},{48,40},{56,48},{64,56},{72,6... | collective-permute-start | bytes 196616 | tf_op jit(solution)/shard_map/ppermute | solution.py:20
  247.7 2.9 collective-permute-start.8
  249.0 3.2 collective-permute-start.9
  256.4 1.3 copy-start.25
  449.1 3.2 copy-start.1
Sparse Core Ops, SparseCore 0:
  131.5 106.5 all-reduce.6
  241.8 194.2 all-reduce.4
